TPU v7x, 512 devices: a whole 4x4x16 slice. The times are simulated.
512 devices in a mesh: lon: 8 (over y, z_hi), mem: 64 (over x, z_lo, core).
Axes of the slice: x: 4, y: 4, z: 16 (z_hi: 2, z_lo: 8; z = z_hi * 8 + z_lo), core: 2. Of those that a mesh axis runs over, the one named last changes fastest.
Arguments:
- ensemble: float32 [64, 98304], P('mem', 'lon')
- increments: bfloat16 [64, 98304], P('mem', 'lon'), may hold values from -6 to 6
- offsets: int32 [192, 7], P('lon'), may hold values from -12 to 12, as said below
- taper: bfloat16 [8, 512, 512], replicated
Outputs:
- covariance_product: float32 [64, 98304], P('mem', 'lon')
Inputs may be any that keep to these rules, and one draw needn't show every extreme that they name: Each row lists 7 different nonzero offsets in ascending order.
All inputs are finite; a program needn't handle non-finite values.
Results may differ from a plain program's by a relative error of at most 0.008.
Values may be sent and summed in bfloat16 or wider, within the bound.
A program may use at most 64 MiB of HBM per device.

v0:
```python
import jax
import jax.numpy as jnp
from jax import lax
from jax.sharding import PartitionSpec as P


def extended_2(block, sides, width):
    for axis, dim in sides:
        count = lax.axis_size(axis)
        forward = [(i, i + 1) for i in range(count - 1)]
        forward.append((count - 1, 0))
        backward = [(target, source) for source, target in forward]
        low = lax.ppermute(
            lax.slice_in_dim(block, block.shape[dim] - width, None, axis=dim), axis, forward
        )
        high = lax.ppermute(lax.slice_in_dim(block, 0, width, axis=dim), axis, backward)
        block = jnp.concatenate([low, block, high], axis=dim)
    return block


def taper_apply(extended, offsets, taper):
    vectors = extended.shape[0]
    block_count = offsets.shape[0]
    block_size = taper.shape[1]
    reach_blocks = block_count // 2
    blocks = extended.reshape(vectors, block_count + 2 * reach_blocks, block_size)
    block_rows = jnp.arange(block_count, dtype=jnp.int32) + reach_blocks
    indices = jnp.concatenate([block_rows[:, None], block_rows[:, None] + offsets], axis=1)
    picked = jnp.take(blocks, indices, axis=1)
    tapered = jnp.einsum("qrsb,sab->qra", picked, taper, preferred_element_type=jnp.float32)
    return tapered.reshape(vectors, block_count * block_size)


def extend_product(factor_one, factor_two, rim_width):
    weighted = (factor_one.astype(jnp.float32) * factor_two.astype(jnp.float32)).astype(
        jnp.bfloat16
    )
    return extended_2(weighted, (("lon", 1),), rim_width)


def on_device(ensemble, increments, offsets, taper):
    member_count = lax.axis_size("mem") * ensemble.shape[0]
    rim_width = offsets.shape[0] // 2 * taper.shape[1]
    ens_mean = lax.psum(jnp.sum(ensemble, axis=0), "mem") / member_count
    perturb = (ensemble - ens_mean[None, :]).astype(jnp.bfloat16)
    increments_all = lax.all_gather(increments, "mem", axis=0, tiled=True)
    extended = extend_product(perturb, increments_all, rim_width)
    tapered = taper_apply(extended, offsets, taper)
    summed = lax.psum_scatter(
        perturb.astype(jnp.float32) * tapered, "mem", scatter_dimension=0, tiled=True
    )
    return summed / (member_count - 1)


def solution(mesh):
    return jax.shard_map(
        on_device,
        mesh=mesh,
        in_specs=(P("mem", "lon"), P("mem", "lon"), P("lon", None), P()),
        out_specs=P("mem", "lon"),
        check_vma=False,
    )
```

profile of v0, /device:TPU:1, one launch (start us, length us, event | category | flops | bytes accessed | tf_op | source)
XLA Modules:
  0.0 1426.9 jit_solution(17073919097878806883)
XLA Ops:
  6.5 0.0 all-gather.3.cloned.1.call-start
  6.5 0.7 all-gather.3.cloned.1.call-update
  7.3 0.0 all-reduce.3.cloned.1.call-start
  7.3 504.5 %psum.7 = f32[12288]{0:T(1024)S(1)} all-reduce(f32[12288]{0:T(1024)} %bitcast.42), channel_id=1, replica_groups=mesh['lon'=8,'mem'=64] {'mem'}, use_global_device_ids=true, to_apply=%region_0.0 | all-reduce | flops 12288 | bytes 98304 | tf_op jit(solution)/shard_map/psum | solution.py:44
  511.9 0.8 convert_convert_fusion
  512.7 0.0 all-gather.3.cloned.1.call-done
  512.7 0.0 copy-start
  512.7 3.6 fusion.6
  516.4 1.3 fusion.14
  517.7 7.0 collective-permute-start
  524.7 9.1 collective-permute-start.1
  533.8 0.0 copy-done
  533.9 0.1 copy.22
  533.9 0.1 reshape.98
  534.1 0.1 copy.19
  534.2 15.4 %collective-permute-done = bf16[64,6144]{1,0:T(8,128)(2,1)S(1)} collective-permute-done((bf16[64,6144]{1,0:T(8,128)(2,1)}, bf16[64,6144]{1,0:T(8,128)(2,1)S(1)}, u32[]{:S(2)}, u32[]{:S(2)}) %collective-permute-start) | collective-permute-done | bytes 786464 | tf_op jit(solution)/shard_map/ppermute | solution.py:13
  549.6 15.8 %collective-permute-done.1 = bf16[64,6144]{1,0:T(8,128)(2,1)S(1)} collective-permute-done((bf16[64,6144]{1,0:T(8,128)(2,1)}, bf16[64,6144]{1,0:T(8,128)(2,1)S(1)}, u32[]{:S(2)}, u32[]{:S(2)}) %collective-permute-start.1) | collective-permute-done | bytes 786464 | tf_op jit(solution)/shard_map/ppermute | solution.py:16
  565.4 0.2 pad_maximum_fusion
  565.6 0.4 copy.30
  566.0 8.2 gather_fusion
  574.2 10.6 fusion.7
  584.9 0.3 copy.27
  585.2 1.9 broadcast_multiply_fusion
  587.1 0.0 all-reduce.3.cloned.1.call-update
  587.2 1.3 dynamic-slice
  588.5 829.2 %all-reduce.3.cloned.1.call-done = f32[64,12288]{1,0:T(8,128)} async-done(((f32[64,12288]{1,0:T(8,128)}), f32[64,12288]{1,0:T(8,128)}) %all-reduce.3.cloned.1.call-update) | async-done | bytes 3145744
  1417.7 2.4 dynamic-slice_multiply_fusion
  (9 shorter events, 0.1 us)
Async XLA Ops:
  6.5 506.2 %all-gather.3.cloned.1.call-start = ((), (), s32[]{:S(2)}) async-start(), calls=%async_computation | async-start | bytes 3194880 | tf_op jit(solution)/shard_map/all_gather | solution.py:46
  7.3 1410.4 %all-reduce.3.cloned.1.call-start = ((), (), s32[]{:S(2)}) async-start(), calls=%async_computation.1 | async-start | bytes 6291456
  512.7 21.1 %copy-start = (s32[24,7]{0,1:T(8,128)S(1)}, s32[24,7]{0,1:T(8,128)}, u32[]{:S(2)}) copy-start(s32[24,7]{0,1:T(8,128)} %param.6) | copy-start | bytes 2020
  517.7 31.9 %collective-permute-start = (bf16[64,6144]{1,0:T(8,128)(2,1)}, bf16[64,6144]{1,0:T(8,128)(2,1)S(1)}, u32[]{:S(2)}, u32[]{:S(2)}) collective-permute-start(bf16[64,6144]{1,0:T(8,128)(2,1)} %get-tuple-element.5), channel_id=1, source_target_pairs={{0,64},{64,128},{128,192},{192,256},{256,320},{320,384},{384,448},... | collective-permute-start | bytes 2359304 | tf_op jit(solution)/shard_map/ppermute | solution.py:13
  524.7 40.6 %collective-permute-start.1 = (bf16[64,6144]{1,0:T(8,128)(2,1)}, bf16[64,6144]{1,0:T(8,128)(2,1)S(1)}, u32[]{:S(2)}, u32[]{:S(2)}) collective-permute-start(bf16[64,6144]{1,0:T(8,128)(2,1)} %get-tuple-element.6), channel_id=1, source_target_pairs={{64,0},{128,64},{192,128},{256,192},{320,256},{384,320},{448,384},... | collective-permute-start | bytes 2359304 | tf_op jit(solution)/shard_map/ppermute | solution.py:16
Sparse Core Ops, SparseCore 0:
  9.5 127.7 all-gather.2
  587.3 830.3 all-reduce.2
where the time goes:
time: 1430 us
  waiting for transfers between devices  861 us (60%)
  blocking collectives  505 us (35%)
  starting transfers between devices  16.1 us (1%)
    unnamed x3, waiting for transfers between devices  830 us
    psum x1, blocking collectives, on_device(): ens_mean = lax.psum(jnp.sum(ensemble, axis=0), 'mem') / member_count  505 us
  transfers between devices with their start and end apart: 4, of which 3 were waited for; matrix products, arithmetic and copies ran while one was open for 0% of the time, Pallas kernels for 0%

commit v1 on v0

--- a/solution.py
+++ b/solution.py
@@ -41,7 +41,7 @@
 def on_device(ensemble, increments, offsets, taper):
     member_count = lax.axis_size("mem") * ensemble.shape[0]
     rim_width = offsets.shape[0] // 2 * taper.shape[1]
-    ens_mean = lax.psum(jnp.sum(ensemble, axis=0), "mem") / member_count
+    ens_mean = jnp.sum(lax.all_gather(jnp.sum(ensemble, axis=0), "mem"), axis=0) / member_count
     perturb = (ensemble - ens_mean[None, :]).astype(jnp.bfloat16)
     increments_all = lax.all_gather(increments, "mem", axis=0, tiled=True)
     extended = extend_product(perturb, increments_all, rim_width)

time: 1430 us -> 1280 us (0.90)
  blocking collectives: 505 us -> 0 us
  waiting for transfers between devices: 861 us -> 1210 us
    psum x1 -> x0, blocking collectives: 505 us -> none  [on_device(): ens_mean = lax.psum(jnp.sum(ensemble, axis=0), 'mem') / member_count]
    all_gather x0 -> x1, waiting for transfers between devices: none -> 129 us  [on_device(): lax.all_gather(jnp.sum(ensemble, axis=0), 'mem')]
    all_gather x1, waiting for transfers between devices: 0.02 us -> 115 us  [on_device(): increments_all = lax.all_gather(increments, 'mem', axis=0, tiled=True)]
    unnamed x3 -> x4, waiting for transfers between devices: 830 us -> 881 us
    ppermute x1, waiting for transfers between devices: 15.8 us -> 51.3 us  [extended_2(): lax.ppermute(lax.slice_in_dim(block, 0, width, axis=dim), axis, backward)]
    ppermute x1, waiting for transfers between devices: 15.4 us -> 34.6 us  [extended_2(): lax.ppermute(lax.slice_in_dim(block, block.shape[dim] - width, None, axis...]
  transfers between devices with their start and end apart: 4 -> 5, of which waited for: 3 -> 5; matrix products, arithmetic and copies ran while one was open for 0% -> 0% of each run, Pallas kernels for 0% -> 0%
where the time goes in v1:
time: 1280 us
  waiting for transfers between devices  1210 us (95%)
  starting transfers between devices  16.2 us (1%)
  between operations  13.2 us (1%)
  other arithmetic  12.8 us (1%)
    unnamed x4, waiting for transfers between devices  881 us
    all_gather x1, waiting for transfers between devices, on_device(): lax.all_gather(jnp.sum(ensemble, axis=0), 'mem')  129 us
    all_gather x1, waiting for transfers between devices, on_device(): increments_all = lax.all_gather(increments, 'mem', axis=0, tiled=True)  115 us
    ppermute x1, waiting for transfers between devices, extended_2(): lax.ppermute(lax.slice_in_dim(block, 0, width, axis=dim), axis, backward)  51.3 us
    ppermute x1, waiting for transfers between devices, extended_2(): lax.ppermute(lax.slice_in_dim(block, block.shape[dim] - width, None, axis...  34.6 us
  transfers between devices with their start and end apart: 5, of which 5 were waited for; matrix products, arithmetic and copies ran while one was open for 0% of the time, Pallas kernels for 0%

profile of v1, /device:TPU:1, one launch (start us, length us, event | category | flops | bytes accessed | tf_op | source)
XLA Modules:
  0.0 1275.7 jit_solution(4548390809056572525)
XLA Ops:
  6.5 0.0 copy-start
  6.5 0.0 all-gather.5.cloned.1.call-start
  6.5 0.7 all-gather.5.cloned.1.call-update
  7.3 0.0 all-gather.7.cloned.1.call-start
  7.3 0.7 all-gather.7.cloned.1.call-update
  8.0 0.0 all-reduce.3.cloned.1.call-start
  8.1 129.3 %all-gather.5.cloned.1.call-done = f32[64,1,12288]{2,1,0:T(1,128)} async-done(((f32[1,1,12288]{2,1,0:T(1,128)}), f32[64,1,12288]{2,1,0:T(1,128)}) %all-gather.5.cloned.1.call-update) | async-done | bytes 3145744 | tf_op jit(solution)/shard_map/all_gather | solution.py:44
  137.4 4.5 reduce_sum.8
  142.0 0.0 copy-done
  142.0 0.1 convert_convert_fusion
  142.0 115.1 %all-gather.7.cloned.1.call-done = bf16[64,1,12288]{2,1,0:T(2,128)(2,1)} async-done(((bf16[1,1,12288]{2,1,0:T(2,128)(2,1)}), bf16[64,1,12288]{2,1,0:T(2,128)(2,1)}) %all-gather.7.cloned.1.call-update) | async-done | bytes 1572880 | tf_op jit(solution)/shard_map/all_gather | solution.py:46
  257.2 0.0 copy-start.1
  257.2 3.6 fusion.6
  260.8 1.3 fusion.14
  262.1 8.4 collective-permute-start
  270.4 7.7 collective-permute-start.1
  278.2 0.0 copy-done.1
  278.2 0.1 copy.22
  278.3 0.1 reshape.108
  278.4 0.1 copy.19
  278.5 34.6 %collective-permute-done = bf16[64,6144]{1,0:T(8,128)(2,1)S(1)} collective-permute-done((bf16[64,6144]{1,0:T(8,128)(2,1)}, bf16[64,6144]{1,0:T(8,128)(2,1)S(1)}, u32[]{:S(2)}, u32[]{:S(2)}) %collective-permute-start) | collective-permute-done | bytes 786464 | tf_op jit(solution)/shard_map/ppermute | solution.py:13
  313.1 51.3 %collective-permute-done.1 = bf16[64,6144]{1,0:T(8,128)(2,1)S(1)} collective-permute-done((bf16[64,6144]{1,0:T(8,128)(2,1)}, bf16[64,6144]{1,0:T(8,128)(2,1)S(1)}, u32[]{:S(2)}, u32[]{:S(2)}) %collective-permute-start.1) | collective-permute-done | bytes 786464 | tf_op jit(solution)/shard_map/ppermute | solution.py:16
  364.4 0.2 pad_maximum_fusion
  364.7 0.4 copy.30
  365.0 8.2 gather_fusion
  373.2 10.6 fusion.7
  383.9 0.3 copy.27
  384.2 1.9 broadcast_multiply_fusion
  386.1 0.0 all-reduce.3.cloned.1.call-update
  386.2 1.3 dynamic-slice
  387.5 879.4 %all-reduce.3.cloned.1.call-done = f32[64,12288]{1,0:T(8,128)} async-done(((f32[64,12288]{1,0:T(8,128)}), f32[64,12288]{1,0:T(8,128)}) %all-reduce.3.cloned.1.call-update) | async-done | bytes 3145744
  1266.9 2.3 dynamic-slice_multiply_fusion
  (9 shorter events, 0.1 us)
Async XLA Ops:
  6.5 135.4 %copy-start = (f32[1,12288]{1,0:T(1,128)S(1)}, f32[1,12288]{1,0:T(1,128)}, u32[]{:S(2)}) copy-start(f32[1,12288]{1,0:T(1,128)} %param.4) | copy-start | bytes 147460
  6.5 130.9 %all-gather.5.cloned.1.call-start = ((), (), s32[]{:S(2)}) async-start(), calls=%async_computation | async-start | bytes 3194880 | tf_op jit(solution)/shard_map/all_gather | solution.py:44
  7.3 249.9 %all-gather.7.cloned.1.call-start = ((), (), s32[]{:S(2)}) async-start(), calls=%async_computation.1 | async-start | bytes 3194880 | tf_op jit(solution)/shard_map/all_gather | solution.py:46
  8.0 1258.9 %all-reduce.3.cloned.1.call-start = ((), (), s32[]{:S(2)}) async-start(), calls=%async_computation.2 | async-start | bytes 6291456
  257.2 21.0 %copy-start.1 = (s32[24,7]{0,1:T(8,128)S(1)}, s32[24,7]{0,1:T(8,128)}, u32[]{:S(2)}) copy-start(s32[24,7]{0,1:T(8,128)} %param.6) | copy-start | bytes 2020
  262.1 51.1 %collective-permute-start = (bf16[64,6144]{1,0:T(8,128)(2,1)}, bf16[64,6144]{1,0:T(8,128)(2,1)S(1)}, u32[]{:S(2)}, u32[]{:S(2)}) collective-permute-start(bf16[64,6144]{1,0:T(8,128)(2,1)} %get-tuple-element.5), channel_id=1, source_target_pairs={{0,64},{64,128},{128,192},{192,256},{256,320},{320,384},{384,448},... | collective-permute-start | bytes 2359304 | tf_op jit(solution)/shard_map/ppermute | solution.py:13
  270.4 94.0 %collective-permute-start.1 = (bf16[64,6144]{1,0:T(8,128)(2,1)}, bf16[64,6144]{1,0:T(8,128)(2,1)S(1)}, u32[]{:S(2)}, u32[]{:S(2)}) collective-permute-start(bf16[64,6144]{1,0:T(8,128)(2,1)} %get-tuple-element.6), channel_id=1, source_target_pairs={{64,0},{128,64},{192,128},{256,192},{320,256},{384,320},{448,384},... | collective-permute-start | bytes 2359304 | tf_op jit(solution)/shard_map/ppermute | solution.py:16
Sparse Core Ops, SparseCore 0:
  9.5 127.8 all-gather.4
  139.5 117.5 all-gather.6
  386.3 880.5 all-reduce.2
